TPU v7x, 32 devices: a whole 2x2x4 slice. The times are simulated.
32 devices in a mesh: groups: 2 (over y), ctx: 4 (over x, core), head: 4 (over z).
Axes of the slice: x: 2, y: 2, z: 4, core: 2. Of those that a mesh axis runs over, the one named last changes fastest.
Arguments:
- queries: bfloat16 [12288, 512], P(('groups', 'ctx', 'head')), parts along dimension 0, may hold values from -8 to 8
- keys: bfloat16 [12288, 512], P(('groups', 'ctx', 'head')), parts along dimension 0, may hold values from -8 to 8
- values: bfloat16 [12288, 512], P(('groups', 'ctx', 'head')), parts along dimension 0, may hold values from -6 to 6
- tile_lists: int32 [96, 16], P(('groups', 'ctx')), parts along dimension 0, may hold values from -8 to 54, as said below
- live_counts: int32 [96], P(('groups', 'ctx')), parts along dimension 0, may hold values from 8 to 16
Outputs:
- attended: bfloat16 [12288, 512], P(('groups', 'ctx', 'head')), parts along dimension 0
There are 2 independent parts, one for each index of `groups`. A program takes and returns all parts, laid end to end along the dimension named above; each array names one. Nothing has to cross between parts.
Inputs may be any that keep to these rules, and one draw needn't show every extreme that they name: `tile_lists`: row t holds t + o for each offset o from -8 to 7 exactly once, the first entry being t itself; entries outside 0 to 47 occur only near the ends of the video.
All inputs are finite; a program needn't handle non-finite values.
Results may differ from a plain program's by a relative error of at most 0.0047.
Values may be sent and summed in bfloat16 or wider, within the bound.
A program may use at most 64 MiB of HBM per device.

v0:
```python
import jax
import jax.numpy as jnp
from jax import lax
from jax.sharding import PartitionSpec as P

HDIM = 128
TILE = 128
EDGE = 8
CTX_TILES = 12
LIST = 16


def with_halo(block, sides, width):
    for axis, dim in sides:
        count = lax.axis_size(axis)
        forward = [(i, i + 1) for i in range(count - 1)]
        backward = [(target, source) for source, target in forward]
        low = lax.ppermute(
            lax.slice_in_dim(block, block.shape[dim] - width, None, axis=dim), axis, forward
        )
        high = lax.ppermute(lax.slice_in_dim(block, 0, width, axis=dim), axis, backward)
        block = jnp.concatenate([low, block, high], axis=dim)
    return block


def block_tiles():
    for candidate in (4, 2, 1):
        return candidate
    return 1


def edge_tiles(kv_pair):
    return with_halo(kv_pair, (("ctx", 1),), EDGE * TILE)


def attend(q_rows, row_lists, row_counts, kv_tiles, query_first, kv_first, total_tiles):
    tile_count = row_lists.shape[0]
    per_block = block_tiles()
    block_count = tile_count // per_block
    window_span = per_block + 2 * EDGE - 1
    score_scale = HDIM ** (-0.5)
    q_blocks = q_rows.reshape(block_count, per_block, TILE, HDIM)
    block_list_entries = row_lists.reshape(block_count, per_block, LIST)
    count_blocks = row_counts.reshape(block_count, per_block)
    block_numbers = jnp.arange(block_count, dtype=jnp.int32)
    positions = jnp.arange(LIST)
    window_steps = jnp.arange(window_span, dtype=jnp.int32)

    def one_block(inputs):
        query_portion, list_part, count_part, block_number = inputs
        block_first = query_first + block_number * per_block
        window_first = block_first - EDGE
        window = lax.dynamic_slice_in_dim(kv_tiles, window_first - kv_first, window_span, 1)
        key_window_tiles = window[0].reshape(window_span * TILE, HDIM)
        value_window_tiles = window[1].reshape(window_span * TILE, HDIM)
        window_ids = window_first + window_steps
        in_range = (window_ids >= 0) & (window_ids < total_tiles)
        live = positions[None, :] < count_part[:, None]
        matched = (list_part[:, :, None] == window_ids[None, None, :]) & live[:, :, None]
        usable = jnp.any(matched, axis=1) & in_range[None, :]
        visible = jnp.repeat(usable, TILE, axis=1)[:, None, :]
        scores = (
            jnp.einsum(
                "tfy,vy->tfv", query_portion, key_window_tiles, preferred_element_type=jnp.float32
            )
            * score_scale
        )
        scores = jnp.where(visible, scores, -1e30)
        highest = jnp.max(scores, axis=-1, keepdims=True)
        weights = jnp.where(visible, jnp.exp(scores - highest), 0.0)
        softmax_divisor = jnp.sum(weights, axis=-1, keepdims=True)
        attention_probs = weights.astype(jnp.bfloat16)
        mixed = jnp.einsum(
            "jzn,nw->jzw", attention_probs, value_window_tiles, preferred_element_type=jnp.float32
        )
        return (mixed / softmax_divisor).astype(jnp.bfloat16)

    results = lax.map(one_block, (q_blocks, block_list_entries, count_blocks, block_numbers))
    return results.reshape(tile_count * TILE, HDIM)


def on_device(queries, keys, values, tile_lists, live_counts):
    ctx_count = lax.axis_size("ctx")
    total_tiles = CTX_TILES * ctx_count
    first_tile = lax.axis_index("ctx") * CTX_TILES
    kv_pair = lax.all_to_all(
        jnp.stack([keys, values]), "head", split_axis=2, concat_axis=1, tiled=True
    )
    padded = edge_tiles(kv_pair)
    local_q = lax.all_to_all(queries, "head", split_axis=1, concat_axis=0, tiled=True)
    padded_count = CTX_TILES + 2 * EDGE
    padded_tiles = padded.reshape(2, padded_count, TILE, HDIM)
    head_out = attend(
        local_q, tile_lists, live_counts, padded_tiles, first_tile, first_tile - EDGE, total_tiles
    )
    return lax.all_to_all(head_out, "head", split_axis=0, concat_axis=1, tiled=True)


def solution(mesh):
    return jax.shard_map(
        on_device,
        mesh=mesh,
        in_specs=(
            P(("groups", "ctx", "head"), None),
            P(("groups", "ctx", "head"), None),
            P(("groups", "ctx", "head"), None),
            P(("groups", "ctx"), None),
            P(("groups", "ctx")),
        ),
        out_specs=P(("groups", "ctx", "head"), None),
        check_vma=False,
    )
```

profile of v0, /device:TPU:0, one launch (start us, length us, event | category | flops | bytes accessed | tf_op | source)
XLA Modules:
  0.0 94.4 jit_solution(12368793994641363082)
XLA Ops:
  0.0 0.0 copy-start
  0.0 1.2 %pad_maximum_fusion.1 = bf16[2,384,512]{2,1,0:T(8,128)(2,1)S(1)} fusion(bf16[1,384,512]{2,1,0:T(8,128)(2,1)} %bitcast.91, bf16[1,384,512]{2,1,0:T(8,128)(2,1)} %bitcast.92), kind=kLoop, calls=%fused_computation.40 | loop fusion | flops 393216 | bytes 1572864 | tf_op jit(solution)/shard_map/stack | solution.py:87
  1.2 1.1 %copy.26 = bf16[2,384,512]{1,0,2:T(2,128)(2,1)S(1)} copy(bf16[2,384,512]{2,1,0:T(8,128)(2,1)S(1)} %pad_maximum_fusion.1) | data formatting | bytes 1572864 | tf_op jit(solution)/shard_map/stack | solution.py:87
  2.4 26.2 %all_to_all.53 = bf16[2,384,512]{1,0,2:T(2,128)(2,1)S(1)} all-to-all(bf16[2,384,512]{1,0,2:T(2,128)(2,1)S(1)} %copy.26), channel_id=1, replica_groups=mesh['groups'=2,'ctx'=4,'head'=4] {'head'}, dimensions={2} | all-to-all | bytes 1572864 | tf_op jit(solution)/shard_map/all_to_all | solution.py:86
  28.6 0.1 copy.27
  28.7 0.4 copy.28
  29.1 0.0 copy-start.1
  29.1 0.0 copy-start.2
  29.1 0.1 fusion.52
  29.2 1.3 %collective-permute-start = (bf16[2,1024,128]{2,1,0:T(8,128)(2,1)S(1)}, bf16[2,1024,128]{2,1,0:T(8,128)(2,1)S(1)}, u32[]{:S(2)}, u32[]{:S(2)}) collective-permute-start(bf16[2,1024,128]{2,1,0:T(8,128)(2,1)S(1)} %get-tuple-element.184), channel_id=1, source_target_pairs={{0,4},{4,8},{8,12},{1,5},{5,9},{9,13},{2,6},{6,10},{10,14},{3,7},{... | collective-permute-start | bytes 1572872 | tf_op jit(solution)/shard_map/ppermute | solution.py:18
  30.5 1.3 %collective-permute-start.1 = (bf16[2,1024,128]{2,1,0:T(8,128)(2,1)S(1)}, bf16[2,1024,128]{2,1,0:T(8,128)(2,1)}, u32[]{:S(2)}, u32[]{:S(2)}) collective-permute-start(bf16[2,1024,128]{2,1,0:T(8,128)(2,1)S(1)} %get-tuple-element.185), channel_id=1, source_target_pairs={{4,0},{8,4},{12,8},{5,1},{9,5},{13,9},{6,2},{10,6},{14,10},{7,3},{... | collective-permute-start | bytes 1572872 | tf_op jit(solution)/shard_map/ppermute | solution.py:21
  31.8 0.0 copy-done
  31.8 0.8 copy_bitcast_fusion.1
  32.7 4.1 %all-to-all-start = ((bf16[384,4,128]{2,0,1:T(8,128)(2,1)}), bf16[384,4,128]{2,0,1:T(8,128)(2,1)}, u32[]{:S(2)}, u32[]{:S(2)}) async-start(bf16[384,4,128]{2,0,1:T(8,128)(2,1)} %copy_bitcast_fusion.1), calls=%async_computation | async-start | bytes 786432 | tf_op jit(solution)/shard_map/all_to_all | solution.py:90
  36.8 0.0 copy-done.1
  36.8 0.0 copy-done.2
  36.8 0.1 reshape.75
  36.9 0.0 collective-permute-done
  36.9 0.0 collective-permute-done.1
  36.9 1.2 %pad_maximum_fusion = bf16[2,3584,128]{2,1,0:T(8,128)(2,1)S(1)} fusion(bf16[2,1024,128]{2,1,0:T(8,128)(2,1)} %collective-permute-done.1, bf16[2,1536,128]{2,1,0:T(8,128)(2,1)S(1)} %bitcast.87, bf16[2,1024,128]{2,1,0:T(8,128)(2,1)S(1)} %collective-permute-done), kind=kLoop, calls=%fused_computation.39 | loop fusion | flops 5505024 | bytes 3670016 | tf_op jit(solution)/shard_map/concatenate | solution.py:22
  38.1 9.7 %all-to-all-done = bf16[384,4,128]{2,0,1:T(8,128)(2,1)} async-done(((bf16[384,4,128]{2,0,1:T(8,128)(2,1)}), bf16[384,4,128]{2,0,1:T(8,128)(2,1)}, u32[]{:S(2)}, u32[]{:S(2)}) %all-to-all-start) | async-done | bytes 393248 | tf_op jit(solution)/shard_map/all_to_all | solution.py:90
  47.8 28.5 %while.13 = (s32[]{:T(128)}, bf16[3,4,128,128]{3,2,1,0:T(8,128)(2,1)}, s32[3,4,16]{2,1,0:T(4,128)S(1)}, s32[3]{0:T(128)S(1)}, s32[]{:T(128)}, /*index=5*/s32[3,4...) while((s32[]{:T(128)}, ...), condition=%wide.region_4.5_spmd.clone, body=%wide.region_0.4_spmd.clone.sunk | while | flops 968893440 | bytes 4826797 | solution.py:78
  47.8 0.6 dynamic_slice.67
  49.1 0.1 constant_dynamic-slice_fusion.4
  49.3 0.1 iota_compare_fusion.2
  49.3 0.1 and_reduce_fusion.2
  49.5 0.1 broadcast_bitcast_fusion.2
  49.6 3.1 %fusion.73 = f32[4,128]{1,0:T(4,128)S(1)} fusion(bf16[2432,128,1]{1,0,2:T(8,128)(2,1)S(1)} %bitcast.83, pred[4,2432]{1,0:T(4,128)(4,1)S(1)} %bitcast.93, bf16[3,4,128,128]{3,2,1,0:T(8,128)(2,1)} %get-tuple-element.281, s32[]{:T(128)} %get-tuple-element.260), kind=kOutput, calls=%fused_computation.42.clone.1 | convolution fusion | flops 324995456 | bytes 775680 | tf_op jit(solution)/shard_map/while/body/eval_jaxpr/sub | solution.py:70
  52.7 4.6 %fusion.74 = bf16[3,4,128,128]{3,2,1,0:T(8,128)(2,1)} fusion(bf16[3,4,128,128]{3,2,1,0:T(8,128)(2,1)} %get-tuple-element.261, s32[]{:T(128)} %get-tuple-element.260, bf16[2432,128,1]{1,0,2:T(8,128)(2,1)S(1)} %bitcast.85, f32[4,128]{1,0:T(4,128)S(1)} %fusion.73, pred[4,2432]{1,0:T(4,128)(4,1)S(1)} %bitcast.94, ...), kind=kOutput, calls=%fused_computation.12.clone.1 | convolution fusion | flops 643894144 | bytes 1529856 | tf_op jit(solution)/shard_map/while/body/eval_jaxpr/jzn,nw->jzw/dot_general | solution.py:73
  57.3 0.6 dynamic_slice.67
  58.6 0.1 constant_dynamic-slice_fusion.4
  58.7 0.1 iota_compare_fusion.2
  58.8 0.1 and_reduce_fusion.2
  58.9 0.1 broadcast_bitcast_fusion.2
  59.0 3.2 %fusion.73 = f32[4,128]{1,0:T(4,128)S(1)} fusion(bf16[2432,128,1]{1,0,2:T(8,128)(2,1)S(1)} %bitcast.83, pred[4,2432]{1,0:T(4,128)(4,1)S(1)} %bitcast.93, bf16[3,4,128,128]{3,2,1,0:T(8,128)(2,1)} %get-tuple-element.281, s32[]{:T(128)} %get-tuple-element.260), kind=kOutput, calls=%fused_computation.42.clone.1 | convolution fusion | flops 324995456 | bytes 775680 | tf_op jit(solution)/shard_map/while/body/eval_jaxpr/sub | solution.py:70
  62.2 4.6 %fusion.74 = bf16[3,4,128,128]{3,2,1,0:T(8,128)(2,1)} fusion(bf16[3,4,128,128]{3,2,1,0:T(8,128)(2,1)} %get-tuple-element.261, s32[]{:T(128)} %get-tuple-element.260, bf16[2432,128,1]{1,0,2:T(8,128)(2,1)S(1)} %bitcast.85, f32[4,128]{1,0:T(4,128)S(1)} %fusion.73, pred[4,2432]{1,0:T(4,128)(4,1)S(1)} %bitcast.94, ...), kind=kOutput, calls=%fused_computation.12.clone.1 | convolution fusion | flops 643894144 | bytes 1529856 | tf_op jit(solution)/shard_map/while/body/eval_jaxpr/jzn,nw->jzw/dot_general | solution.py:73
  66.8 0.6 dynamic_slice.67
  68.0 0.1 constant_dynamic-slice_fusion.4
  68.2 0.1 iota_compare_fusion.2
  68.3 0.1 and_reduce_fusion.2
  68.4 0.1 broadcast_bitcast_fusion.2
  68.5 3.2 %fusion.73 = f32[4,128]{1,0:T(4,128)S(1)} fusion(bf16[2432,128,1]{1,0,2:T(8,128)(2,1)S(1)} %bitcast.83, pred[4,2432]{1,0:T(4,128)(4,1)S(1)} %bitcast.93, bf16[3,4,128,128]{3,2,1,0:T(8,128)(2,1)} %get-tuple-element.281, s32[]{:T(128)} %get-tuple-element.260), kind=kOutput, calls=%fused_computation.42.clone.1 | convolution fusion | flops 324995456 | bytes 775680 | tf_op jit(solution)/shard_map/while/body/eval_jaxpr/sub | solution.py:70
  71.7 4.6 %fusion.74 = bf16[3,4,128,128]{3,2,1,0:T(8,128)(2,1)} fusion(bf16[3,4,128,128]{3,2,1,0:T(8,128)(2,1)} %get-tuple-element.261, s32[]{:T(128)} %get-tuple-element.260, bf16[2432,128,1]{1,0,2:T(8,128)(2,1)S(1)} %bitcast.85, f32[4,128]{1,0:T(4,128)S(1)} %fusion.73, pred[4,2432]{1,0:T(4,128)(4,1)S(1)} %bitcast.94, ...), kind=kOutput, calls=%fused_computation.12.clone.1 | convolution fusion | flops 643894144 | bytes 1529856 | tf_op jit(solution)/shard_map/while/body/eval_jaxpr/jzn,nw->jzw/dot_general | solution.py:73
  76.3 16.9 %all_to_all.54 = bf16[4,384,128]{2,1,0:T(8,128)(2,1)S(1)} all-to-all(bf16[4,384,128]{2,1,0:T(8,128)(2,1)} %bitcast.90), channel_id=1, replica_groups=mesh['groups'=2,'ctx'=4,'head'=4] {'head'}, dimensions={0} | all-to-all | bytes 786432 | tf_op jit(solution)/shard_map/all_to_all | solution.py:96
  93.2 0.2 copy.29
  93.5 0.9 copy.30
  (21 shorter events, 0.2 us)
Async XLA Ops:
  0.0 31.8 %copy-start = (bf16[384,512]{1,0:T(8,128)(2,1)S(1)}, bf16[384,512]{1,0:T(8,128)(2,1)}, u32[]{:S(2)}) copy-start(bf16[384,512]{1,0:T(8,128)(2,1)} %param.7) | copy-start | bytes 1179652
  29.1 7.7 %copy-start.1 = (s32[12,16]{1,0:T(8,128)S(1)}, s32[12,16]{1,0:T(8,128)}, u32[]{:S(2)}) copy-start(s32[12,16]{1,0:T(8,128)} %param.10) | copy-start | bytes 2308
  29.1 7.7 %copy-start.2 = (s32[12]{0:T(128)S(1)}, s32[12]{0:T(128)}, u32[]{:S(2)}) copy-start(s32[12]{0:T(128)} %param.11) | copy-start | bytes 148
  29.2 7.7 %collective-permute-start = (bf16[2,1024,128]{2,1,0:T(8,128)(2,1)S(1)}, bf16[2,1024,128]{2,1,0:T(8,128)(2,1)S(1)}, u32[]{:S(2)}, u32[]{:S(2)}) collective-permute-start(bf16[2,1024,128]{2,1,0:T(8,128)(2,1)S(1)} %get-tuple-element.184), channel_id=1, source_target_pairs={{0,4},{4,8},{8,12},{1,5},{5,9},{9,13},{2,6},{6,10},{10,14},{3,7},{... | collective-permute-start | bytes 1572872 | tf_op jit(solution)/shard_map/ppermute | solution.py:18
  30.5 6.4 %collective-permute-start.1 = (bf16[2,1024,128]{2,1,0:T(8,128)(2,1)S(1)}, bf16[2,1024,128]{2,1,0:T(8,128)(2,1)}, u32[]{:S(2)}, u32[]{:S(2)}) collective-permute-start(bf16[2,1024,128]{2,1,0:T(8,128)(2,1)S(1)} %get-tuple-element.185), channel_id=1, source_target_pairs={{4,0},{8,4},{12,8},{5,1},{9,5},{13,9},{6,2},{10,6},{14,10},{7,3},{... | collective-permute-start | bytes 1572872 | tf_op jit(solution)/shard_map/ppermute | solution.py:21
  32.7 15.2 %all-to-all-start = ((bf16[384,4,128]{2,0,1:T(8,128)(2,1)}), bf16[384,4,128]{2,0,1:T(8,128)(2,1)}, u32[]{:S(2)}, u32[]{:S(2)}) async-start(bf16[384,4,128]{2,0,1:T(8,128)(2,1)} %copy_bitcast_fusion.1), calls=%async_computation | async-start | bytes 786432 | tf_op jit(solution)/shard_map/all_to_all | solution.py:90
where the time goes:
time: 94.9 us; the launch traced here: 94.4 us
  blocking collectives  43.2 us (46%)
  matrix products  23.3 us (25%)
  waiting for transfers between devices  9.74 us (10%)
  starting transfers between devices  6.73 us (7%)
  local copies, waits for them, and re-layouts  6.34 us (7%)
  other arithmetic  2.97 us (3%)
  loops' own time  2.05 us (2%)
    all_to_all x1, blocking collectives, on_device(): lax.all_to_all(jnp.stack([keys, values]), 'head', split_axis=2, concat_ax...  26.2 us
    all_to_all x1, blocking collectives, on_device(): lax.all_to_all(head_out, 'head', split_axis=0, concat_axis=1, tiled=True)  16.9 us
    dot_general x3, matrix products, one_block(): jnp.einsum('jzn,nw->jzw', attention_probs, value_window_tiles, preferred_...  13.8 us
    all_to_all x1, waiting for transfers between devices, on_device(): lax.all_to_all(queries, 'head', split_axis=1, concat_axis=0, tiled=True)  9.74 us
    sub x3, matrix products, one_block(): weights = jnp.where(visible, jnp.exp(scores - highest), 0.0)  9.46 us
    all_to_all x1, starting transfers between devices, on_device(): lax.all_to_all(queries, 'head', split_axis=1, concat_axis=0, tiled=True)  4.11 us
    another operation x1, loops' own time, attend(): lax.map(one_block, (q_blocks, block_list_entries, count_blocks, block_num...  2.05 us
  transfers between devices with their start and end apart: 3, of which 1 were waited for; matrix products, arithmetic and copies ran while one was open for 2% of the time, Pallas kernels for 0%

commit v1 on v0

--- a/solution.py
+++ b/solution.py
@@ -8,6 +8,28 @@
 EDGE = 8
 CTX_TILES = 12
 LIST = 16
+
+
+def in_blocks(shard, dim, size):
+    before, after = (shard.shape[:dim], shard.shape[dim + 1 :])
+    return jnp.moveaxis(shard.reshape(*before, size, -1, *after), dim, 0)
+
+
+def in_order(blocks, dim):
+    blocks = jnp.moveaxis(blocks, 0, dim)
+    lengths = blocks.shape
+    return blocks.reshape(*lengths[:dim], lengths[dim] * lengths[dim + 1], *lengths[dim + 2 :])
+
+
+def exchange_in_pairs(array, axis, split_dim, concat_dim):
+    size, index = (lax.axis_size(axis), lax.axis_index(axis))
+    blocks = in_blocks(array, split_dim, size)
+    outs = [blocks[index]]
+    for step in range(1, size):
+        sent = blocks[index ^ step]
+        outs.append(lax.ppermute(sent, axis, [(i, i ^ step) for i in range(size)]))
+    blocks = jnp.stack(outs)[index ^ jnp.arange(size)]
+    return in_order(blocks, concat_dim)
 
 
 def with_halo(block, sides, width):
@@ -87,7 +109,7 @@
         jnp.stack([keys, values]), "head", split_axis=2, concat_axis=1, tiled=True
     )
     padded = edge_tiles(kv_pair)
-    local_q = lax.all_to_all(queries, "head", split_axis=1, concat_axis=0, tiled=True)
+    local_q = exchange_in_pairs(queries, "head", 1, 0)
     padded_count = CTX_TILES + 2 * EDGE
     padded_tiles = padded.reshape(2, padded_count, TILE, HDIM)
     head_out = attend(

time: 94.9 us -> 91.6 us (0.965)
  waiting for transfers between devices: 9.74 us -> 4.3 us
  local copies, waits for them, and re-layouts: 6.34 us -> 8.41 us
  matrix products: 23.3 us -> 21.4 us
    all_to_all x1 -> x0, waiting for transfers between devices: 9.74 us -> none  [on_device(): lax.all_to_all(queries, 'head', split_axis=1, concat_axis=0, tiled=True)]
    ppermute x0 -> x3, starting transfers between devices: none -> 4.58 us  [exchange_in_pairs(): outs.append(lax.ppermute(sent, axis, [(i, i ^ step) for i in range(size)]))]
    ppermute x0 -> x3, waiting for transfers between devices: none -> 4.3 us  [exchange_in_pairs(): outs.append(lax.ppermute(sent, axis, [(i, i ^ step) for i in range(size)]))]
    all_to_all x1 -> x0, starting transfers between devices: 4.11 us -> none  [on_device(): lax.all_to_all(queries, 'head', split_axis=1, concat_axis=0, tiled=True)]
    dot_general x3, matrix products: 13.8 us -> 12 us  [one_block(): jnp.einsum('jzn,nw->jzw', attention_probs, value_window_tiles, preferred_...]
    gather x0 -> x1, local copies, waits for them, and re-layouts: none -> 1.34 us  [exchange_in_pairs(): blocks = jnp.stack(outs)[index ^ jnp.arange(size)]]
  transfers between devices with their start and end apart: 3 -> 5, of which waited for: 1 -> 2; matrix products, arithmetic and copies ran while one was open for 2% -> 4% of each run, Pallas kernels for 0% -> 0%
where the time goes in v1:
time: 91.6 us; the launch traced here: 91.1 us
  blocking collectives  43.4 us (47%)
  matrix products  21.4 us (23%)
  local copies, waits for them, and re-layouts  8.41 us (9%)
  starting transfers between devices  7.2 us (8%)
  waiting for transfers between devices  4.3 us (5%)
  other arithmetic  3.87 us (4%)
  loops' own time  2.35 us (3%)
    all_to_all x1, blocking collectives, on_device(): lax.all_to_all(jnp.stack([keys, values]), 'head', split_axis=2, concat_ax...  26.2 us
    all_to_all x1, blocking collectives, on_device(): lax.all_to_all(head_out, 'head', split_axis=0, concat_axis=1, tiled=True)  17.1 us
    dot_general x3, matrix products, one_block(): jnp.einsum('jzn,nw->jzw', attention_probs, value_window_tiles, preferred_...  12 us
    sub x3, matrix products, one_block(): weights = jnp.where(visible, jnp.exp(scores - highest), 0.0)  9.45 us
    ppermute x3, starting transfers between devices, exchange_in_pairs(): outs.append(lax.ppermute(sent, axis, [(i, i ^ step) for i in range(size)]))  4.58 us
    ppermute x3, waiting for transfers between devices, exchange_in_pairs(): outs.append(lax.ppermute(sent, axis, [(i, i ^ step) for i in range(size)]))  4.3 us
    another operation x1, loops' own time, attend(): lax.map(one_block, (q_blocks, block_list_entries, count_blocks, block_num...  2.35 us
    dynamic_slice x3, local copies, waits for them, and re-layouts, attend(): lax.map(one_block, (q_blocks, block_list_entries, count_blocks, block_num...  2 us
  transfers between devices with their start and end apart: 5, of which 2 were waited for; matrix products, arithmetic and copies ran while one was open for 4% of the time, Pallas kernels for 0%

profile of v1, /device:TPU:0, one launch (start us, length us, event | category | flops | bytes accessed | tf_op | source)
XLA Modules:
  0.0 91.1 jit_solution(3516511065728472409)
XLA Ops:
  0.0 1.2 %pad_maximum_fusion.1 = bf16[2,384,512]{2,1,0:T(8,128)(2,1)S(1)} fusion(bf16[1,384,512]{2,1,0:T(8,128)(2,1)} %bitcast.96, bf16[1,384,512]{2,1,0:T(8,128)(2,1)} %bitcast.97), kind=kLoop, calls=%fused_computation.41 | loop fusion | flops 393216 | bytes 1572864 | tf_op jit(solution)/shard_map/stack | solution.py:109
  1.2 1.1 %copy.47 = bf16[2,384,512]{1,0,2:T(2,128)(2,1)S(1)} copy(bf16[2,384,512]{2,1,0:T(8,128)(2,1)S(1)} %pad_maximum_fusion.1) | data formatting | bytes 1572864 | tf_op jit(solution)/shard_map/stack | solution.py:109
  2.3 26.2 %all_to_all.37 = bf16[2,384,512]{1,0,2:T(2,128)(2,1)S(1)} all-to-all(bf16[2,384,512]{1,0,2:T(2,128)(2,1)S(1)} %copy.47), channel_id=1, replica_groups=mesh['groups'=2,'ctx'=4,'head'=4] {'head'}, dimensions={2} | all-to-all | bytes 1572864 | tf_op jit(solution)/shard_map/all_to_all | solution.py:108
  28.6 0.1 copy.48
  28.7 0.0 copy-start
  28.7 0.4 copy.49
  29.1 0.0 copy-start.1
  29.1 0.1 fusion.53
  29.1 1.3 %collective-permute-start.3 = (bf16[2,1024,128]{2,1,0:T(8,128)(2,1)S(1)}, bf16[2,1024,128]{2,1,0:T(8,128)(2,1)S(1)}, u32[]{:S(2)}, u32[]{:S(2)}) collective-permute-start(bf16[2,1024,128]{2,1,0:T(8,128)(2,1)S(1)} %get-tuple-element.184), channel_id=1, source_target_pairs={{0,4},{4,8},{8,12},{1,5},{5,9},{9,13},{2,6},{6,10},{10,14},{3,7},{... | collective-permute-start | bytes 1572872 | tf_op jit(solution)/shard_map/ppermute | solution.py:40
  30.5 1.3 %collective-permute-start.4 = (bf16[2,1024,128]{2,1,0:T(8,128)(2,1)S(1)}, bf16[2,1024,128]{2,1,0:T(8,128)(2,1)}, u32[]{:S(2)}, u32[]{:S(2)}) collective-permute-start(bf16[2,1024,128]{2,1,0:T(8,128)(2,1)S(1)} %get-tuple-element.185), channel_id=1, source_target_pairs={{4,0},{8,4},{12,8},{5,1},{9,5},{13,9},{6,2},{10,6},{14,10},{7,3},{... | collective-permute-start | bytes 1572872 | tf_op jit(solution)/shard_map/ppermute | solution.py:43
  31.8 0.0 copy-done
  31.8 0.2 copy.42
  32.0 0.1 constant_dynamic-slice_fusion.6
  32.1 0.1 copy.44
  32.2 0.3 collective-permute-start
  32.5 0.1 copy.45
  32.6 1.9 %collective-permute-start.1 = (bf16[384,128]{1,0:T(8,128)(2,1)S(1)}, bf16[384,128]{1,0:T(8,128)(2,1)S(1)}, u32[]{:S(2)}, u32[]{:S(2)}) collective-permute-start(bf16[384,128]{1,0:T(8,128)(2,1)S(1)} %bitcast.104), channel_id=1, source_target_pairs={{0,2},{1,3},{2,0},{3,1},{4,6},{5,7},{6,4},{7,5},{8,10},{9,11},{10,... | collective-permute-start | bytes 294920 | tf_op jit(solution)/shard_map/ppermute | solution.py:30
  34.5 0.1 copy.46
  34.6 2.4 %collective-permute-start.2 = (bf16[384,128]{1,0:T(8,128)(2,1)S(1)}, bf16[384,128]{1,0:T(8,128)(2,1)}, u32[]{:S(2)}, u32[]{:S(2)}) collective-permute-start(bf16[384,128]{1,0:T(8,128)(2,1)S(1)} %bitcast.105), channel_id=1, source_target_pairs={{0,3},{1,2},{2,1},{3,0},{4,7},{5,6},{6,5},{7,4},{8,11},{9,10},{10,... | collective-permute-start | bytes 294920 | tf_op jit(solution)/shard_map/ppermute | solution.py:30
  37.1 0.1 copy.43
  37.2 0.0 copy-done.1
  37.2 0.7 reshape.94
  38.0 0.0 collective-permute-done
  38.0 0.3 collective-permute-done.1
  38.3 4.0 %collective-permute-done.2 = bf16[384,128]{1,0:T(8,128)(2,1)} collective-permute-done((bf16[384,128]{1,0:T(8,128)(2,1)S(1)}, bf16[384,128]{1,0:T(8,128)(2,1)}, u32[]{:S(2)}, u32[]{:S(2)}) %collective-permute-start.2) | collective-permute-done | bytes 98336 | tf_op jit(solution)/shard_map/ppermute | solution.py:30
  42.3 0.9 %pad_maximum_fusion.2 = bf16[4,384,128]{2,1,0:T(8,128)(2,1)S(1)} fusion(bf16[1,384,128]{2,1,0:T(8,128)(2,1)} %bitcast.7, bf16[1,384,128]{2,1,0:T(8,128)(2,1)S(1)} %bitcast.102, bf16[1,384,128]{2,1,0:T(8,128)(2,1)S(1)} %bitcast.101, bf16[1,384,128]{2,1,0:T(8,128)(2,1)S(1)} %bitcast.95), kind=kLoop, calls=%fused_computation.42 | loop fusion | flops 589824 | bytes 786432 | tf_op jit(solution)/shard_map/stack | solution.py:31
  43.2 1.3 %gather_fusion = bf16[4,384,128]{2,1,0:T(8,128)(2,1)} fusion(bf16[4,384,128]{2,1,0:T(8,128)(2,1)S(1)} %pad_maximum_fusion.2, s32[1024]{0:T(1024)S(1)} %pad_clamp_fusion), kind=kCustom, calls=%fused_computation | custom fusion | bytes 786448 | tf_op jit(solution)/shard_map/gather | solution.py:31
  44.6 0.0 collective-permute-done.3
  44.6 0.0 collective-permute-done.4
  44.6 1.2 %pad_maximum_fusion = bf16[2,3584,128]{2,1,0:T(8,128)(2,1)S(1)} fusion(bf16[2,1024,128]{2,1,0:T(8,128)(2,1)} %collective-permute-done.4, bf16[2,1536,128]{2,1,0:T(8,128)(2,1)S(1)} %bitcast.90, bf16[2,1024,128]{2,1,0:T(8,128)(2,1)S(1)} %collective-permute-done.3), kind=kLoop, calls=%fused_computation.40 | loop fusion | flops 5505024 | bytes 3670016 | tf_op jit(solution)/shard_map/concatenate | solution.py:44
  45.7 27.1 %while.13 = (s32[]{:T(128)}, bf16[3,4,128,128]{3,2,1,0:T(8,128)(2,1)S(1)}, s32[3,4,16]{2,1,0:T(4,128)S(1)}, s32[3]{0:T(128)S(1)}, s32[]{:T(128)}, /*index=5*/s32...) while((s32[]{:T(128)}, ...), condition=%wide.region_4.5_spmd.clone, body=%wide.region_0.4_spmd.clone.sunk | while | flops 968893440 | bytes 4826797 | solution.py:100
  45.8 0.7 dynamic_slice.74
  47.1 0.1 constant_dynamic-slice_fusion.8
  47.3 0.1 iota_compare_fusion.2
  47.4 0.1 and_reduce_fusion.2
  47.5 0.1 broadcast_bitcast_fusion.2
  47.6 3.1 %fusion.73 = f32[4,128]{1,0:T(4,128)S(1)} fusion(bf16[2432,128,1]{1,0,2:T(8,128)(2,1)S(1)} %bitcast.86, pred[4,2432]{1,0:T(4,128)(4,1)S(1)} %bitcast.99, bf16[3,4,128,128]{3,2,1,0:T(8,128)(2,1)} %get-tuple-element.285, s32[]{:T(128)} %get-tuple-element.264), kind=kOutput, calls=%fused_computation.50.clone.1 | convolution fusion | flops 324995456 | bytes 775680 | tf_op jit(solution)/shard_map/while/body/eval_jaxpr/sub | solution.py:92
  50.8 4.0 %fusion.74 = bf16[3,4,128,128]{3,2,1,0:T(8,128)(2,1)S(1)} fusion(bf16[3,4,128,128]{3,2,1,0:T(8,128)(2,1)S(1)} %get-tuple-element.265, s32[]{:T(128)} %get-tuple-element.264, bf16[2432,128,1]{1,0,2:T(8,128)(2,1)S(1)} %bitcast.88, f32[4,128]{1,0:T(4,128)S(1)} %fusion.73, pred[4,2432]{1,0:T(4,128)(4,1)S(1)} %bitcast.100, ...), kind=kOutput, calls=%fused_computation.13.clone.1 | convolution fusion | flops 643894144 | bytes 1529856 | tf_op jit(solution)/shard_map/while/body/eval_jaxpr/jzn,nw->jzw/dot_general | solution.py:95
  54.8 0.7 dynamic_slice.74
  56.2 0.1 constant_dynamic-slice_fusion.8
  56.3 0.1 iota_compare_fusion.2
  56.4 0.1 and_reduce_fusion.2
  56.5 0.1 broadcast_bitcast_fusion.2
  56.6 3.1 %fusion.73 = f32[4,128]{1,0:T(4,128)S(1)} fusion(bf16[2432,128,1]{1,0,2:T(8,128)(2,1)S(1)} %bitcast.86, pred[4,2432]{1,0:T(4,128)(4,1)S(1)} %bitcast.99, bf16[3,4,128,128]{3,2,1,0:T(8,128)(2,1)} %get-tuple-element.285, s32[]{:T(128)} %get-tuple-element.264), kind=kOutput, calls=%fused_computation.50.clone.1 | convolution fusion | flops 324995456 | bytes 775680 | tf_op jit(solution)/shard_map/while/body/eval_jaxpr/sub | solution.py:92
  59.8 4.0 %fusion.74 = bf16[3,4,128,128]{3,2,1,0:T(8,128)(2,1)S(1)} fusion(bf16[3,4,128,128]{3,2,1,0:T(8,128)(2,1)S(1)} %get-tuple-element.265, s32[]{:T(128)} %get-tuple-element.264, bf16[2432,128,1]{1,0,2:T(8,128)(2,1)S(1)} %bitcast.88, f32[4,128]{1,0:T(4,128)S(1)} %fusion.73, pred[4,2432]{1,0:T(4,128)(4,1)S(1)} %bitcast.100, ...), kind=kOutput, calls=%fused_computation.13.clone.1 | convolution fusion | flops 643894144 | bytes 1529856 | tf_op jit(solution)/shard_map/while/body/eval_jaxpr/jzn,nw->jzw/dot_general | solution.py:95
  63.8 0.7 dynamic_slice.74
  65.2 0.1 constant_dynamic-slice_fusion.8
  65.4 0.1 iota_compare_fusion.2
  65.4 0.1 and_reduce_fusion.2
  65.6 0.1 broadcast_bitcast_fusion.2
  65.7 3.2 %fusion.73 = f32[4,128]{1,0:T(4,128)S(1)} fusion(bf16[2432,128,1]{1,0,2:T(8,128)(2,1)S(1)} %bitcast.86, pred[4,2432]{1,0:T(4,128)(4,1)S(1)} %bitcast.99, bf16[3,4,128,128]{3,2,1,0:T(8,128)(2,1)} %get-tuple-element.285, s32[]{:T(128)} %get-tuple-element.264), kind=kOutput, calls=%fused_computation.50.clone.1 | convolution fusion | flops 324995456 | bytes 775680 | tf_op jit(solution)/shard_map/while/body/eval_jaxpr/sub | solution.py:92
  68.8 4.0 %fusion.74 = bf16[3,4,128,128]{3,2,1,0:T(8,128)(2,1)S(1)} fusion(bf16[3,4,128,128]{3,2,1,0:T(8,128)(2,1)S(1)} %get-tuple-element.265, s32[]{:T(128)} %get-tuple-element.264, bf16[2432,128,1]{1,0,2:T(8,128)(2,1)S(1)} %bitcast.88, f32[4,128]{1,0:T(4,128)S(1)} %fusion.73, pred[4,2432]{1,0:T(4,128)(4,1)S(1)} %bitcast.100, ...), kind=kOutput, calls=%fused_computation.13.clone.1 | convolution fusion | flops 643894144 | bytes 1529856 | tf_op jit(solution)/shard_map/while/body/eval_jaxpr/jzn,nw->jzw/dot_general | solution.py:95
  72.8 17.1 %all_to_all.38 = bf16[4,384,128]{2,1,0:T(8,128)(2,1)S(1)} all-to-all(bf16[4,384,128]{2,1,0:T(8,128)(2,1)S(1)} %bitcast.94), channel_id=1, replica_groups=mesh['groups'=2,'ctx'=4,'head'=4] {'head'}, dimensions={0} | all-to-all | bytes 786432 | tf_op jit(solution)/shard_map/all_to_all | solution.py:118
  90.0 0.2 copy.50
  90.2 0.9 %copy.51 = bf16[384,512]{1,0:T(8,128)(2,1)} copy(bf16[384,512]{0,1:T(8,128)(2,1)S(1)} %bitcast.93) | data formatting | bytes 786432 | tf_op jit(solution)/shard_map/all_to_all | solution.py:118
  (23 shorter events, 0.2 us)
Async XLA Ops:
  28.7 3.1 %copy-start = (bf16[384,512]{1,0:T(8,128)(2,1)S(1)}, bf16[384,512]{1,0:T(8,128)(2,1)}, u32[]{:S(2)}) copy-start(bf16[384,512]{1,0:T(8,128)(2,1)} %param.7) | copy-start | bytes 1179652
  29.1 8.1 %copy-start.1 = (s32[12,16]{1,0:T(8,128)S(1)}, s32[12,16]{1,0:T(8,128)}, u32[]{:S(2)}) copy-start(s32[12,16]{1,0:T(8,128)} %param.10) | copy-start | bytes 2308
  29.1 15.4 %collective-permute-start.3 = (bf16[2,1024,128]{2,1,0:T(8,128)(2,1)S(1)}, bf16[2,1024,128]{2,1,0:T(8,128)(2,1)S(1)}, u32[]{:S(2)}, u32[]{:S(2)}) collective-permute-start(bf16[2,1024,128]{2,1,0:T(8,128)(2,1)S(1)} %get-tuple-element.184), channel_id=1, source_target_pairs={{0,4},{4,8},{8,12},{1,5},{5,9},{9,13},{2,6},{6,10},{10,14},{3,7},{... | collective-permute-start | bytes 1572872 | tf_op jit(solution)/shard_map/ppermute | solution.py:40
  30.5 14.1 %collective-permute-start.4 = (bf16[2,1024,128]{2,1,0:T(8,128)(2,1)S(1)}, bf16[2,1024,128]{2,1,0:T(8,128)(2,1)}, u32[]{:S(2)}, u32[]{:S(2)}) collective-permute-start(bf16[2,1024,128]{2,1,0:T(8,128)(2,1)S(1)} %get-tuple-element.185), channel_id=1, source_target_pairs={{4,0},{8,4},{12,8},{5,1},{9,5},{13,9},{6,2},{10,6},{14,10},{7,3},{... | collective-permute-start | bytes 1572872 | tf_op jit(solution)/shard_map/ppermute | solution.py:43
  32.2 5.7 %collective-permute-start = (bf16[384,128]{1,0:T(8,128)(2,1)S(1)}, bf16[384,128]{1,0:T(8,128)(2,1)S(1)}, u32[]{:S(2)}, u32[]{:S(2)}) collective-permute-start(bf16[384,128]{1,0:T(8,128)(2,1)S(1)} %bitcast.103), channel_id=1, source_target_pairs={{0,1},{1,0},{2,3},{3,2},{4,5},{5,4},{6,7},{7,6},{8,9},{9,8},{10,11... | collective-permute-start | bytes 294920 | tf_op jit(solution)/shard_map/ppermute | solution.py:30
  32.6 5.6 %collective-permute-start.1 = (bf16[384,128]{1,0:T(8,128)(2,1)S(1)}, bf16[384,128]{1,0:T(8,128)(2,1)S(1)}, u32[]{:S(2)}, u32[]{:S(2)}) collective-permute-start(bf16[384,128]{1,0:T(8,128)(2,1)S(1)} %bitcast.104), channel_id=1, source_target_pairs={{0,2},{1,3},{2,0},{3,1},{4,6},{5,7},{6,4},{7,5},{8,10},{9,11},{10,... | collective-permute-start | bytes 294920 | tf_op jit(solution)/shard_map/ppermute | solution.py:30
  34.6 7.6 %collective-permute-start.2 = (bf16[384,128]{1,0:T(8,128)(2,1)S(1)}, bf16[384,128]{1,0:T(8,128)(2,1)}, u32[]{:S(2)}, u32[]{:S(2)}) collective-permute-start(bf16[384,128]{1,0:T(8,128)(2,1)S(1)} %bitcast.105), channel_id=1, source_target_pairs={{0,3},{1,2},{2,1},{3,0},{4,7},{5,6},{6,5},{7,4},{8,11},{9,10},{10,... | collective-permute-start | bytes 294920 | tf_op jit(solution)/shard_map/ppermute | solution.py:30
